TPU v7x, 32 devices: a whole 2x2x4 slice. The times are simulated.
32 devices in a mesh: groups: 2 (over y), cols: 4 (over z), rows: 4 (over x, core).
Axes of the slice: x: 2, y: 2, z: 4, core: 2. Of those that a mesh axis runs over, the one named last changes fastest.
Arguments:
- acts: bfloat16 [4, 257, 1536], P('groups', None, 'rows'), parts along dimension 0, may hold values from -6 to 6
- out_grad: bfloat16 [4, 257, 1536], P('groups', None, 'rows'), parts along dimension 0, may hold values from -0.59765625 to 0.59765625
- w_in: bfloat16 [1536, 6144], P(None, 'cols'), may hold values from -0.15625 to 0.15625
- bias_in: bfloat16 [6144], P('cols'), may hold values from -4 to 4
- w_out: bfloat16 [6144, 1536], P('cols'), may hold values from -0.15625 to 0.15625
- sign_bits: int32 [16777216], P(('cols', 'rows')), may hold values 0 or 1
- picks: int32 [4096], replicated, may hold values from 0 to 16777215, as said below
Outputs:
- sketch: float32 [4, 4096], P('groups'), parts along dimension 0
There are 2 independent parts, one for each index of `groups`. A program takes and returns all parts, laid end to end along the dimension named above; an argument that names none is the same for every part. Nothing has to cross between parts.
Inputs may be any that keep to these rules, and one draw needn't show every extreme that they name: `picks`: 4096 distinct positions in increasing order; the first is 0 and the last is 16777215.
All inputs are finite; a program needn't handle non-finite values. No bound on the sum of `sign_bits` on one device may be relied on, other than what follows from the above.
Results may differ from a plain program's by a relative error of at most 0.0031.
Values may be sent and summed in bfloat16 or wider, within the bound.
A program may use at most 192 MiB of HBM per device.

v0:
```python
import functools
import math

import jax
import jax.numpy as jnp
from jax import lax
from jax.experimental import pallas as pl
from jax.experimental.pallas import tpu as pltpu
from jax.sharding import PartitionSpec as P

root_half = 0.7071067811865476
inv_root_two_pi = 0.3989422804014327
LANES = 128
MESH = pl.DeviceIdType.MESH


def gelu_slope(inputs):
    normal_cdf = 0.5 * (1.0 + lax.erf(inputs * root_half))
    return normal_cdf + inputs * inv_root_two_pi * jnp.exp(-0.5 * inputs * inputs)


def signs_of(left, right):
    odd = jnp.bitwise_and(lax.population_count(jnp.bitwise_and(left, right)), 1)
    return (1 - 2 * odd).astype(jnp.float32)


def low_part(hidden_part):
    return hidden_part & -hidden_part


def plain_body(acts, out_grad, w_in, bias_in, w_out, sign_bits, picks):
    images, tokens, width_part = acts.shape
    hidden_part = w_in.shape[1]
    low_len = low_part(hidden_part)
    act_all = lax.all_gather(acts, "rows", axis=2, tiled=True)
    grad_all = lax.all_gather(out_grad, "rows", axis=2, tiled=True)
    pre_act = jnp.einsum("itd,df->itf", act_all, w_in, preferred_element_type=jnp.float32)
    pre_act = pre_act + bias_in.astype(jnp.float32)
    back = jnp.einsum("itd,fd->itf", grad_all, w_out, preferred_element_type=jnp.float32)
    pre_grad = (back * gelu_slope(pre_act)).astype(jnp.bfloat16)
    weight_grad = jnp.einsum("itd,itf->idf", acts, pre_grad, preferred_element_type=jnp.float32)
    local_len = sign_bits.shape[0]
    used = width_part * hidden_part
    flips = (1 - 2 * sign_bits[:used]).astype(jnp.float32)
    signed = (weight_grad.reshape(images, used) * flips).astype(jnp.bfloat16)
    signed = signed.reshape(images, used // low_len, low_len)
    inside = picks % local_len
    high_signs = signs_of((inside // low_len)[:, None], jnp.arange(used // low_len)[None, :])
    low_signs = signs_of((inside % low_len)[:, None], jnp.arange(low_len)[None, :])
    half = jnp.einsum(
        "mq,iql->iml", high_signs.astype(jnp.bfloat16), signed, preferred_element_type=jnp.float32
    )
    shards = lax.axis_size(("cols", "rows"))
    me = lax.axis_index(("cols", "rows"))
    contrib = jnp.sum(half * low_signs[None], axis=2) * signs_of(picks // local_len, me)[None, :]
    return lax.psum(contrib, ("cols", "rows")) * (1.0 / math.sqrt(local_len * shards))


def kernel(
    local_len,
    blocks_hbm,
    w_in_hbm,
    bias_ref,
    w_out_hbm,
    bits_hbm,
    picks_ref,
    out_ref,
    blocks,
    w_in,
    w_out,
    bits,
    high,
    low,
    signed,
    sems,
):
    row_shards, _, tokens, width = blocks.shape
    hidden = w_in.shape[1]
    low_len = low.shape[1]
    groups = hidden // low_len
    images = out_ref.shape[0]
    image_rows = tokens // images
    me_row = lax.axis_index("rows")
    me_all = lax.axis_index("cols") * lax.axis_size("rows") + me_row
    copies = [
        pltpu.make_async_copy(blocks_hbm, blocks, sems.at[0]),
        pltpu.make_async_copy(w_in_hbm, w_in, sems.at[1]),
        pltpu.make_async_copy(w_out_hbm, w_out, sems.at[2]),
        pltpu.make_async_copy(bits_hbm.at[pl.ds(0, bits.shape[0])], bits, sems.at[3]),
    ]
    for copy in copies:
        copy.start()

    lane = lax.broadcasted_iota(jnp.int32, (LANES, LANES), 1)

    def make_signs(at, _):
        column = jnp.broadcast_to(picks_ref[pl.ds(at, 1), :], (LANES, LANES)).T
        inside = jnp.bitwise_and(column, local_len - 1)
        upper = jnp.right_shift(inside, low_len.bit_length() - 1)
        lower = jnp.bitwise_and(inside, low_len - 1)
        rows = pl.ds(pl.multiple_of(at * LANES, LANES), LANES)
        for group in range(groups):
            for tile in range(width // LANES):
                place = groups * (lane + tile * LANES) + group
                start = group * width + tile * LANES
                high[rows, start : start + LANES] = signs_of(upper, place).astype(jnp.bfloat16)
        for tile in range(low_len // LANES):
            low[rows, tile * LANES : (tile + 1) * LANES] = signs_of(
                lower, lane + tile * LANES
            ).astype(jnp.bfloat16)
        return 0

    lax.fori_loop(0, picks_ref.shape[0], make_signs, 0)
    for copy in copies:
        copy.wait()

    for group in range(groups):
        cols = slice(group * low_len, (group + 1) * low_len)
        pre = jnp.broadcast_to(bias_ref[:, cols].astype(jnp.float32), (tokens, low_len))
        back = jnp.zeros((tokens, low_len), jnp.float32)
        for row in range(row_shards):
            part = slice(row * width, (row + 1) * width)
            pre = pre + jnp.dot(
                blocks[row, 0], w_in[part, cols], preferred_element_type=jnp.float32
            )
            back = back + lax.dot_general(
                blocks[row, 1],
                w_out[cols, part],
                (((1,), (1,)), ((), ())),
                preferred_element_type=jnp.float32,
            )
        pre_grad = (back * gelu_slope(pre)).astype(jnp.bfloat16)
        for image in range(images):
            rows = slice(image * image_rows, (image + 1) * image_rows)
            grad = lax.dot_general(
                blocks[me_row, 0, rows, :],
                pre_grad[rows],
                (((0,), (0,)), ((), ())),
                preferred_element_type=jnp.float32,
            )
            for tile in range(low_len // LANES):
                first = group * (low_len // LANES) + tile
                flips = bits[pl.ds(first, width, stride=hidden // LANES), :]
                piece = grad[:, tile * LANES : (tile + 1) * LANES]
                start = image * low_len + tile * LANES
                signed[group * width : (group + 1) * width, start : start + LANES] = (
                    piece * (1 - 2 * flips).astype(jnp.float32)
                ).astype(jnp.bfloat16)

    scale = 1.0 / math.sqrt(local_len * lax.axis_size("cols") * row_shards)
    step = 2 * LANES

    def select(at, _):
        rows = pl.ds(pl.multiple_of(at * step, step), step)
        half = jnp.dot(high[rows, :], signed[...], preferred_element_type=jnp.float32)
        weight = low[rows, :].astype(jnp.float32)
        for image in range(images):
            total = jnp.zeros((step, LANES), jnp.float32)
            for tile in range(low_len // LANES):
                start = image * low_len + tile * LANES
                total = total + half[:, start : start + LANES] * weight[
                    :, tile * LANES : (tile + 1) * LANES
                ]
            for part in range(2):
                block = total[part * LANES : (part + 1) * LANES].T
                out_ref[image, pl.ds(2 * at + part, 1), :] = jnp.sum(block, axis=0, keepdims=True)
        return 0

    lax.fori_loop(0, picks_ref.shape[0] // 2, select, 0)
    owner = jnp.right_shift(picks_ref[...], local_len.bit_length() - 1)
    facing = signs_of(owner, jnp.broadcast_to(me_all, owner.shape)) * scale
    for image in range(images):
        out_ref[image] = out_ref[image] * facing


def body(acts, out_grad, w_in, bias_in, w_out, sign_bits, picks):
    images, tokens, width = acts.shape
    hidden = w_in.shape[1]
    low_len = low_part(hidden)
    if low_len % LANES or width % LANES or picks.shape[0] % (16 * LANES):
        return plain_body(acts, out_grad, w_in, bias_in, w_out, sign_bits, picks)
    row_shards = lax.axis_size("rows")
    local_len = sign_bits.shape[0]
    padded = -(-tokens // 16) * 16
    own = jnp.pad(jnp.stack([acts, out_grad]), ((0, 0), (0, 0), (0, padded - tokens), (0, 0)))
    own = own.reshape(2, images * padded, width)
    blocks = lax.all_gather(own, "rows", axis=0, tiled=False)
    groups = hidden // low_len
    count = picks.shape[0]
    contrib = pl.pallas_call(
        functools.partial(kernel, local_len),
        out_shape=jax.ShapeDtypeStruct((images, count // LANES, LANES), jnp.float32),
        in_specs=[
            pl.BlockSpec(memory_space=pl.ANY),
            pl.BlockSpec(memory_space=pl.ANY),
            pl.BlockSpec(memory_space=pltpu.VMEM),
            pl.BlockSpec(memory_space=pl.ANY),
            pl.BlockSpec(memory_space=pl.ANY),
            pl.BlockSpec(memory_space=pltpu.VMEM),
        ],
        out_specs=pl.BlockSpec(memory_space=pltpu.VMEM),
        scratch_shapes=[
            pltpu.VMEM((row_shards, 2, images * padded, width), jnp.bfloat16),
            pltpu.VMEM(w_in.shape, jnp.bfloat16),
            pltpu.VMEM(w_out.shape, jnp.bfloat16),
            pltpu.VMEM((width * hidden // LANES, LANES), jnp.int32),
            pltpu.VMEM((count, groups * width), jnp.bfloat16),
            pltpu.VMEM((count, low_len), jnp.bfloat16),
            pltpu.VMEM((groups * width, images * low_len), jnp.bfloat16),
            pltpu.SemaphoreType.DMA((4,)),
        ],
        compiler_params=pltpu.CompilerParams(vmem_limit_bytes=56 * 2**20),
    )(
        blocks,
        w_in,
        bias_in.reshape(1, hidden),
        w_out,
        sign_bits.reshape(local_len // LANES, LANES),
        picks.reshape(count // LANES, LANES),
    )
    return lax.psum(contrib, ("cols", "rows")).reshape(images, count)


def solution(mesh):
    return jax.shard_map(
        body,
        mesh=mesh,
        in_specs=(
            P("groups", None, "rows"),
            P("groups", None, "rows"),
            P(None, "cols"),
            P("cols"),
            P("cols", None),
            P(("cols", "rows")),
            P(),
        ),
        out_specs=P("groups", None),
        check_vma=False,
    )
```

profile of v0, /device:TPU:0, one launch (start us, length us, event | category | flops | bytes accessed | tf_op | source)
XLA Modules:
  0.0 145.0 jit_solution(16259385001565501387)
XLA Ops:
  6.5 0.0 copy-start
  6.5 0.0 all-gather.2.cloned.1.call-start
  6.5 2.3 %pad_maximum_fusion = bf16[2,2,257,384]{3,1,2,0:T(2,128)(2,1)S(1)} fusion(bf16[1,2,257,384]{3,1,2,0:T(2,128)(2,1)} %bitcast.11, bf16[1,2,257,384]{3,1,2,0:T(2,128)(2,1)} %bitcast.12), kind=kLoop, calls=%fused_computation | loop fusion | flops 394752 | bytes 1579008 | tf_op jit(solution)/shard_map/stack | solution.py:185
  8.8 0.1 copy.10
  9.0 1.0 pad.4.clone
  10.0 0.0 all-gather.2.cloned.1.call-update
  10.0 0.0 copy-done
  10.0 0.6 reshape.12.bias_ref
  10.6 31.9 %all-gather.2.cloned.1.call-done.blocks_hbm = bf16[4,2,544,384]{3,2,1,0:T(8,128)(2,1)} async-done(((bf16[1,2,544,384]{3,2,1,0:T(8,128)(2,1)}), bf16[4,2,544,384]{3,2,1,0:T(8,128)(2,1)}) %all-gather.2.cloned.1.call-update) | async-done | bytes 3342352 | tf_op jit(solution)/shard_map/all_gather | solution.py:187
  42.5 33.6 %shard_map.73 = f32[2,32,128]{2,1,0:T(8,128)} custom-call(bf16[4,2,544,384]{3,2,1,0:T(8,128)(2,1)} %all-gather.2.cloned.1.call-done.blocks_hbm, bf16[1536,1536]{1,0:T(8,128)(2,1)} %w_in_hbm.1, bf16[1,1536]{1,0:T(2,128)(2,1)} %reshape.12.bias_ref, bf16[1536,1536]{1,0:T(8,128)(2,1)} %w_out_hbm.1, s32[8192,128]{1,0:T(8,128)} %bitcast.9, s32[32,128]{1,0:T(8,128)} %bitcast.15), custom_call_target="tpu_custom_call" | custom-call | tf_op jit(solution)/shard_map/pallas_call | solution.py:190
  76.1 0.8 copy.13
  76.9 61.3 %psum.7 = f32[2,4096]{1,0:T(2,128)} all-reduce(f32[2,4096]{1,0:T(2,128)S(1)} %bitcast.14), channel_id=1, replica_groups=mesh['groups'=2,'cols'=4,'rows'=4] {'cols','rows'}, use_global_device_ids=true, to_apply=%region_0.1 | all-reduce | flops 8192 | bytes 65536 | tf_op jit(solution)/shard_map/psum | solution.py:221
Async XLA Ops:
  6.5 3.5 %copy-start = (bf16[1536]{0:T(1024)(128)(2,1)S(1)}, bf16[1536]{0:T(1024)(128)(2,1)}, u32[]{:S(2)}) copy-start(bf16[1536]{0:T(1024)(128)(2,1)} %param.10) | copy-start | bytes 9220
  6.5 36.0 %all-gather.2.cloned.1.call-start = ((), (), s32[]{:S(2)}) async-start(), calls=%async_computation | async-start | bytes 4177920 | tf_op jit(solution)/shard_map/all_gather | solution.py:187
Sparse Core Ops, SparseCore 0:
  10.1 32.3 all-gather.1
where the time goes:
time: 145 us
  blocking collectives  61.3 us (42%)
  Pallas kernels  33.6 us (23%)
  waiting for transfers between devices  31.9 us (22%)
  between operations  13.4 us (9%)
  local copies, waits for them, and re-layouts  2.5 us (2%)
  other arithmetic  2.3 us (2%)
    psum x1, blocking collectives, body(): return lax.psum(contrib, ('cols', 'rows')).reshape(images, count)  61.3 us
    pallas_call x1, Pallas kernels, body(): pl.pallas_call(functools.partial(kernel, local_len), out_shape=jax.ShapeD...  33.6 us
    all_gather x1, waiting for transfers between devices, body(): blocks = lax.all_gather(own, 'rows', axis=0, tiled=False)  31.9 us
  transfers between devices with their start and end apart: 1, of which 1 were waited for; matrix products, arithmetic and copies ran while one was open for 0% of the time, Pallas kernels for 0%

commit v1 on v0

--- a/solution.py
+++ b/solution.py
@@ -58,7 +58,9 @@
 
 def kernel(
     local_len,
-    blocks_hbm,
+    col_shards,
+    acts_ref,
+    grads_ref,
     w_in_hbm,
     bias_ref,
     w_out_hbm,
@@ -72,24 +74,100 @@
     high,
     low,
     signed,
-    sems,
+    pre_sum,
+    back_sum,
+    mixed,
+    incoming,
+    load_sems,
+    twin_sems,
+    far_sems,
+    layer_sems,
+    pass_far_sems,
+    pass_layer_sems,
+    sum_sems,
 ):
-    row_shards, _, tokens, width = blocks.shape
+    images, tokens, width = acts_ref.shape
+    image_rows = blocks.shape[1] // images
     hidden = w_in.shape[1]
     low_len = low.shape[1]
     groups = hidden // low_len
-    images = out_ref.shape[0]
-    image_rows = tokens // images
-    me_row = lax.axis_index("rows")
-    me_all = lax.axis_index("cols") * lax.axis_size("rows") + me_row
-    copies = [
-        pltpu.make_async_copy(blocks_hbm, blocks, sems.at[0]),
-        pltpu.make_async_copy(w_in_hbm, w_in, sems.at[1]),
-        pltpu.make_async_copy(w_out_hbm, w_out, sems.at[2]),
-        pltpu.make_async_copy(bits_hbm.at[pl.ds(0, bits.shape[0])], bits, sems.at[3]),
+    row_shards = 4
+    row = lax.axis_index("rows")
+    col = lax.axis_index("cols")
+    me_all = col * row_shards + row
+
+    twin = row + 1 - 2 * lax.rem(row, 2)
+    far = lax.rem(row + 2, row_shards)
+    partners = [{"rows": twin}, {"rows": far}]
+    hop = 1
+    while hop < col_shards:
+        partners.append({"cols": col + hop - 2 * hop * lax.rem(col // hop, 2)})
+        hop *= 2
+    layer = partners[2]
+
+    barrier = pltpu.get_barrier_semaphore()
+    for partner in partners:
+        pl.semaphore_signal(barrier, inc=1, device_id=partner, device_id_type=MESH)
+
+    loads = [
+        pltpu.make_async_copy(bits_hbm.at[pl.ds(0, bits.shape[0])], bits, load_sems.at[0]),
+        pltpu.make_async_copy(w_in_hbm, w_in, load_sems.at[1]),
+        pltpu.make_async_copy(w_out_hbm, w_out, load_sems.at[2]),
     ]
-    for copy in copies:
+    for load in loads[1:] + loads[:1]:
+        load.start()
+
+    own_cols = pl.ds(pl.multiple_of(row * width, LANES), width)
+    gap = jnp.zeros((image_rows - tokens, width), jnp.bfloat16)
+    for image in range(images):
+        for kind, ref in enumerate((acts_ref, grads_ref)):
+            blocks[kind, image * image_rows : (image + 1) * image_rows, own_cols] = (
+                jnp.concatenate([ref[image], gap], axis=0)
+            )
+    pl.semaphore_wait(barrier, len(partners))
+
+    tiles = images * image_rows // 16
+    count = far_sems.shape[1]
+    edges = [16 * (tiles * part // count) for part in range(count + 1)]
+
+    def place(kind, owner, part):
+        rows = pl.ds(0, images * image_rows)
+        if part is not None:
+            rows = pl.ds(edges[part], edges[part + 1] - edges[part])
+        return blocks.at[kind, rows, pl.ds(pl.multiple_of(owner * width, LANES), width)]
+
+    def send(ref, sems, at, partner):
+        return pltpu.make_async_remote_copy(
+            src_ref=ref,
+            dst_ref=ref,
+            send_sem=sems.at[0, at],
+            recv_sem=sems.at[1, at],
+            device_id=partner,
+            device_id_type=MESH,
+        )
+
+    mine = lax.rem(col, 2)
+    to_far = [send(place(mine, row, part), far_sems, part, partners[1]) for part in range(count)]
+    to_twin = [send(place(kind, row, None), twin_sems, kind, partners[0]) for kind in range(2)]
+    to_layer = [send(place(mine, far, part), layer_sems, part, layer) for part in range(count)]
+    pass_far = [
+        send(place(mine, far, part), pass_far_sems, part, partners[0]) for part in range(count)
+    ]
+    pass_layer = [
+        send(place(1 - mine, far, part), pass_layer_sems, part, partners[0])
+        for part in range(count)
+    ]
+    for copy in to_far + to_twin:
         copy.start()
+
+    def relay_far(part):
+        to_far[part].wait_recv()
+        to_layer[part].start()
+        pass_far[part].start()
+
+    def relay_layer(part):
+        to_layer[part].wait_recv()
+        pass_layer[part].start()
 
     lane = lax.broadcasted_iota(jnp.int32, (LANES, LANES), 1)
 
@@ -101,39 +179,74 @@
         rows = pl.ds(pl.multiple_of(at * LANES, LANES), LANES)
         for group in range(groups):
             for tile in range(width // LANES):
-                place = groups * (lane + tile * LANES) + group
+                spot = groups * (lane + tile * LANES) + group
                 start = group * width + tile * LANES
-                high[rows, start : start + LANES] = signs_of(upper, place).astype(jnp.bfloat16)
+                high[rows, start : start + LANES] = signs_of(upper, spot).astype(jnp.bfloat16)
         for tile in range(low_len // LANES):
             low[rows, tile * LANES : (tile + 1) * LANES] = signs_of(
                 lower, lane + tile * LANES
             ).astype(jnp.bfloat16)
         return 0
 
-    lax.fori_loop(0, picks_ref.shape[0], make_signs, 0)
-    for copy in copies:
-        copy.wait()
+    def signs(part):
+        every = picks_ref.shape[0]
+        lax.fori_loop(every * part // 4, every * (part + 1) // 4, make_signs, 0)
+
+    pair = 2 * width
+
+    def products(half, group):
+        cols = slice(group * low_len, (group + 1) * low_len)
+        part = pl.ds(pl.multiple_of(half * pair, LANES), pair)
+        pre = jnp.dot(blocks[0, :, part], w_in[part, cols], preferred_element_type=jnp.float32)
+        back = lax.dot_general(
+            blocks[1, :, part],
+            w_out[cols, part],
+            (((1,), (1,)), ((), ())),
+            preferred_element_type=jnp.float32,
+        )
+        return pre, back
+
+    here = row // 2
+
+    def own_products(group):
+        cols = slice(group * low_len, (group + 1) * low_len)
+        pre, back = products(here, group)
+        pre_sum[:, cols] = pre + bias_ref[:, cols].astype(jnp.float32)
+        back_sum[:, cols] = back
+
+    signs(0)
+    signs(1)
+    relay_far(0)
+    signs(2)
+    relay_far(1)
+    signs(3)
+    relay_layer(0)
+    relay_far(2)
+    for load in loads[1:]:
+        load.wait()
+    for copy in to_twin:
+        copy.wait_recv()
+    own_products(0)
+    relay_far(3)
+    relay_layer(1)
+    for group in range(1, groups):
+        own_products(group)
+    relay_layer(2)
+    relay_layer(3)
+    loads[0].wait()
+    for copy in pass_far + pass_layer:
+        copy.wait_recv()
 
     for group in range(groups):
         cols = slice(group * low_len, (group + 1) * low_len)
-        pre = jnp.broadcast_to(bias_ref[:, cols].astype(jnp.float32), (tokens, low_len))
-        back = jnp.zeros((tokens, low_len), jnp.float32)
-        for row in range(row_shards):
-            part = slice(row * width, (row + 1) * width)
-            pre = pre + jnp.dot(
-                blocks[row, 0], w_in[part, cols], preferred_element_type=jnp.float32
-            )
-            back = back + lax.dot_general(
-                blocks[row, 1],
-                w_out[cols, part],
-                (((1,), (1,)), ((), ())),
-                preferred_element_type=jnp.float32,
-            )
+        pre, back = products(1 - here, group)
+        pre = pre + pre_sum[:, cols]
+        back = back + back_sum[:, cols]
         pre_grad = (back * gelu_slope(pre)).astype(jnp.bfloat16)
         for image in range(images):
             rows = slice(image * image_rows, (image + 1) * image_rows)
             grad = lax.dot_general(
-                blocks[me_row, 0, rows, :],
+                blocks[0, rows, own_cols],
                 pre_grad[rows],
                 (((0,), (0,)), ((), ())),
                 preferred_element_type=jnp.float32,
@@ -147,7 +260,6 @@
                     piece * (1 - 2 * flips).astype(jnp.float32)
                 ).astype(jnp.bfloat16)
 
-    scale = 1.0 / math.sqrt(local_len * lax.axis_size("cols") * row_shards)
     step = 2 * LANES
 
     def select(at, _):
@@ -163,62 +275,91 @@
                 ]
             for part in range(2):
                 block = total[part * LANES : (part + 1) * LANES].T
-                out_ref[image, pl.ds(2 * at + part, 1), :] = jnp.sum(block, axis=0, keepdims=True)
+                mixed[image, pl.ds(2 * at + part, 1), :] = jnp.sum(block, axis=0, keepdims=True)
         return 0
 
     lax.fori_loop(0, picks_ref.shape[0] // 2, select, 0)
+    scale = 1.0 / math.sqrt(local_len * col_shards * row_shards)
     owner = jnp.right_shift(picks_ref[...], local_len.bit_length() - 1)
     facing = signs_of(owner, jnp.broadcast_to(me_all, owner.shape)) * scale
     for image in range(images):
-        out_ref[image] = out_ref[image] * facing
+        mixed[image] = mixed[image] * facing
+
+    for at, partner in enumerate(partners):
+        copy = pltpu.make_async_remote_copy(
+            src_ref=mixed,
+            dst_ref=incoming.at[at],
+            send_sem=sum_sems.at[0, at],
+            recv_sem=sum_sems.at[1, at],
+            device_id=partner,
+            device_id_type=MESH,
+        )
+        copy.start()
+        copy.wait()
+        if at < len(partners) - 1:
+            mixed[...] = mixed[...] + incoming[at]
+        else:
+            out_ref[...] = mixed[...] + incoming[at]
+    for copy in to_far + to_twin + to_layer + pass_far + pass_layer:
+        copy.wait_send()
 
 
 def body(acts, out_grad, w_in, bias_in, w_out, sign_bits, picks):
     images, tokens, width = acts.shape
     hidden = w_in.shape[1]
     low_len = low_part(hidden)
-    if low_len % LANES or width % LANES or picks.shape[0] % (16 * LANES):
+    row_shards = lax.axis_size("rows")
+    col_shards = lax.axis_size("cols")
+    fits = low_len % LANES == 0 and width % LANES == 0 and picks.shape[0] % (16 * LANES) == 0
+    if not fits or row_shards != 4 or col_shards < 2 or col_shards & (col_shards - 1):
         return plain_body(acts, out_grad, w_in, bias_in, w_out, sign_bits, picks)
-    row_shards = lax.axis_size("rows")
     local_len = sign_bits.shape[0]
     padded = -(-tokens // 16) * 16
-    own = jnp.pad(jnp.stack([acts, out_grad]), ((0, 0), (0, 0), (0, padded - tokens), (0, 0)))
-    own = own.reshape(2, images * padded, width)
-    blocks = lax.all_gather(own, "rows", axis=0, tiled=False)
     groups = hidden // low_len
     count = picks.shape[0]
-    contrib = pl.pallas_call(
-        functools.partial(kernel, local_len),
-        out_shape=jax.ShapeDtypeStruct((images, count // LANES, LANES), jnp.float32),
-        in_specs=[
-            pl.BlockSpec(memory_space=pl.ANY),
-            pl.BlockSpec(memory_space=pl.ANY),
-            pl.BlockSpec(memory_space=pltpu.VMEM),
-            pl.BlockSpec(memory_space=pl.ANY),
-            pl.BlockSpec(memory_space=pl.ANY),
-            pl.BlockSpec(memory_space=pltpu.VMEM),
-        ],
-        out_specs=pl.BlockSpec(memory_space=pltpu.VMEM),
+    parts = 4
+    steps = 1 + col_shards.bit_length()
+    sketch_shape = (images, count // LANES, LANES)
+    vmem = pl.BlockSpec(memory_space=pltpu.VMEM)
+    anywhere = pl.BlockSpec(memory_space=pl.ANY)
+    sketch = pl.pallas_call(
+        functools.partial(kernel, local_len, col_shards),
+        out_shape=jax.ShapeDtypeStruct(sketch_shape, jnp.float32),
+        in_specs=[vmem, vmem, anywhere, vmem, anywhere, anywhere, vmem],
+        out_specs=vmem,
         scratch_shapes=[
-            pltpu.VMEM((row_shards, 2, images * padded, width), jnp.bfloat16),
+            pltpu.VMEM((2, images * padded, row_shards * width), jnp.bfloat16),
             pltpu.VMEM(w_in.shape, jnp.bfloat16),
             pltpu.VMEM(w_out.shape, jnp.bfloat16),
             pltpu.VMEM((width * hidden // LANES, LANES), jnp.int32),
             pltpu.VMEM((count, groups * width), jnp.bfloat16),
             pltpu.VMEM((count, low_len), jnp.bfloat16),
             pltpu.VMEM((groups * width, images * low_len), jnp.bfloat16),
-            pltpu.SemaphoreType.DMA((4,)),
+            pltpu.VMEM((images * padded, hidden), jnp.float32),
+            pltpu.VMEM((images * padded, hidden), jnp.float32),
+            pltpu.VMEM(sketch_shape, jnp.float32),
+            pltpu.VMEM((steps,) + sketch_shape, jnp.float32),
+            pltpu.SemaphoreType.DMA((3,)),
+            pltpu.SemaphoreType.DMA((2, 2)),
+            pltpu.SemaphoreType.DMA((2, parts)),
+            pltpu.SemaphoreType.DMA((2, parts)),
+            pltpu.SemaphoreType.DMA((2, parts)),
+            pltpu.SemaphoreType.DMA((2, parts)),
+            pltpu.SemaphoreType.DMA((2, steps)),
         ],
-        compiler_params=pltpu.CompilerParams(vmem_limit_bytes=56 * 2**20),
+        compiler_params=pltpu.CompilerParams(
+            vmem_limit_bytes=56 * 2**20, collective_id=0, has_side_effects=True
+        ),
     )(
-        blocks,
+        acts,
+        out_grad,
         w_in,
         bias_in.reshape(1, hidden),
         w_out,
         sign_bits.reshape(local_len // LANES, LANES),
         picks.reshape(count // LANES, LANES),
     )
-    return lax.psum(contrib, ("cols", "rows")).reshape(images, count)
+    return sketch.reshape(images, count)
 
 
 def solution(mesh):

time: 145 us -> 58.5 us (0.40)
  blocking collectives: 61.3 us -> 0 us
  waiting for transfers between devices: 31.9 us -> 0 us
  Pallas kernels: 33.6 us -> 52 us
  between operations: 13.4 us -> 0.01 us
  local copies, waits for them, and re-layouts: 2.5 us -> 6.26 us
  other arithmetic: 2.3 us -> 0 us
    psum x1 -> x0, blocking collectives: 61.3 us -> none  [body(): return lax.psum(contrib, ('cols', 'rows')).reshape(images, count)]
    all_gather x1 -> x0, waiting for transfers between devices: 31.9 us -> none  [body(): blocks = lax.all_gather(own, 'rows', axis=0, tiled=False)]
    pallas_call x1, Pallas kernels: 33.6 us -> 52 us  [body(): pl.pallas_call(functools.partial(kernel, local_len, col_shards), out_shap...]
    unnamed x4 -> x3, local copies, waits for them, and re-layouts: 0.9 us -> 4.97 us
    another operation x1 -> x0, other arithmetic: 2.3 us -> none  [body(): jnp.stack([acts, out_grad])]
  transfers between devices with their start and end apart: 1 -> 0, of which waited for: 1 -> 0; matrix products, arithmetic and copies ran while one was open for 0% -> 0% of each run, Pallas kernels for 0% -> 0%
where the time goes in v1:
time: 58.5 us; the launch traced here: 58.2 us
  Pallas kernels  52 us (89%)
  local copies, waits for them, and re-layouts  6.26 us (11%)
    pallas_call x1, Pallas kernels, body(): pl.pallas_call(functools.partial(kernel, local_len, col_shards), out_shap...  52 us
    unnamed x3, local copies, waits for them, and re-layouts  4.97 us
    reshape x1, local copies, waits for them, and re-layouts, body(): bias_in.reshape(1, hidden)  1.28 us

profile of v1, /device:TPU:0, one launch (start us, length us, event | category | flops | bytes accessed | tf_op | source)
XLA Modules:
  0.0 58.2 jit_solution(3848608743687322659)
XLA Ops:
  0.0 1.3 %reshape.12.bias_ref = bf16[1,1536]{1,0:T(2,128)(2,1)} reshape(bf16[1536]{0:T(1024)(128)(2,1)} %param.10) | data formatting | bytes 6144 | tf_op jit(solution)/shard_map/reshape | solution.py:357
  1.3 1.8 %copy.8.acts_ref = bf16[2,257,384]{2,1,0:T(8,128)(2,1)} copy(bf16[2,257,384]{2,0,1:T(2,128)(2,1)} %param.7) | data formatting | bytes 789504 | tf_op args[0]
  3.1 1.8 %copy.9.grads_ref = bf16[2,257,384]{2,1,0:T(8,128)(2,1)} copy(bf16[2,257,384]{2,0,1:T(2,128)(2,1)} %param.8) | data formatting | bytes 789504 | tf_op args[1]
  4.9 52.0 %shard_map.73 = f32[2,32,128]{2,1,0:T(8,128)} custom-call(bf16[2,257,384]{2,1,0:T(8,128)(2,1)} %copy.8.acts_ref, bf16[2,257,384]{2,1,0:T(8,128)(2,1)} %copy.9.grads_ref, bf16[1536,1536]{1,0:T(8,128)(2,1)} %w_in_hbm.1, bf16[1,1536]{1,0:T(2,128)(2,1)} %reshape.12.bias_ref, bf16[1536,1536]{1,0:T(8,128)(2,1)} %w_out_hbm.1, s32[8192,128]{1,0:T(8,128)} %bitcast.6, ...), custom_call_target="tpu_custom_call" | custom-call | tf_op jit(solution)/shard_map/pallas_call | solution.py:325
  56.8 1.4 %copy.12 = f32[1,2,32,128]{3,1,2,0:T(2,128)} copy(f32[1,2,32,128]{3,2,1,0:T(8,128)} %bitcast.7) | data formatting | bytes 65536

commit v2 on v1

v2 whole, which is shorter than its diff:
```python
import functools
import math

import jax
import jax.numpy as jnp
from jax import lax
from jax.experimental import pallas as pl
from jax.experimental.pallas import tpu as pltpu
from jax.sharding import PartitionSpec as P

root_half = 0.7071067811865476
inv_root_two_pi = 0.3989422804014327
LANES = 128
MESH = pl.DeviceIdType.MESH


def gelu_slope(inputs):
    normal_cdf = 0.5 * (1.0 + lax.erf(inputs * root_half))
    return normal_cdf + inputs * inv_root_two_pi * jnp.exp(-0.5 * inputs * inputs)


def signs_of(left, right):
    odd = jnp.bitwise_and(lax.population_count(jnp.bitwise_and(left, right)), 1)
    return (1 - 2 * odd).astype(jnp.float32)


def low_part(hidden_part):
    return hidden_part & -hidden_part


def plain_body(acts, out_grad, w_in, bias_in, w_out, sign_bits, picks):
    images, tokens, width_part = acts.shape
    hidden_part = w_in.shape[1]
    low_len = low_part(hidden_part)
    act_all = lax.all_gather(acts, "rows", axis=2, tiled=True)
    grad_all = lax.all_gather(out_grad, "rows", axis=2, tiled=True)
    pre_act = jnp.einsum("itd,df->itf", act_all, w_in, preferred_element_type=jnp.float32)
    pre_act = pre_act + bias_in.astype(jnp.float32)
    back = jnp.einsum("itd,fd->itf", grad_all, w_out, preferred_element_type=jnp.float32)
    pre_grad = (back * gelu_slope(pre_act)).astype(jnp.bfloat16)
    weight_grad = jnp.einsum("itd,itf->idf", acts, pre_grad, preferred_element_type=jnp.float32)
    local_len = sign_bits.shape[0]
    used = width_part * hidden_part
    flips = (1 - 2 * sign_bits[:used]).astype(jnp.float32)
    signed = (weight_grad.reshape(images, used) * flips).astype(jnp.bfloat16)
    signed = signed.reshape(images, used // low_len, low_len)
    inside = picks % local_len
    high_signs = signs_of((inside // low_len)[:, None], jnp.arange(used // low_len)[None, :])
    low_signs = signs_of((inside % low_len)[:, None], jnp.arange(low_len)[None, :])
    half = jnp.einsum(
        "mq,iql->iml", high_signs.astype(jnp.bfloat16), signed, preferred_element_type=jnp.float32
    )
    shards = lax.axis_size(("cols", "rows"))
    me = lax.axis_index(("cols", "rows"))
    contrib = jnp.sum(half * low_signs[None], axis=2) * signs_of(picks // local_len, me)[None, :]
    return lax.psum(contrib, ("cols", "rows")) * (1.0 / math.sqrt(local_len * shards))


def kernel(
    local_len,
    col_shards,
    acts_hbm,
    grads_hbm,
    w_in_hbm,
    bias_ref,
    w_out_hbm,
    bits_hbm,
    picks_ref,
    out_ref,
    raw,
    blocks,
    w_in,
    w_out,
    bits,
    high,
    low,
    signed,
    pre_sum,
    back_sum,
    mixed,
    row_slots,
    col_slots,
    load_sems,
    twin_sems,
    far_sems,
    layer_sems,
    pass_far_sems,
    pass_layer_sems,
    row_sems,
    col_sems,
):
    images, tokens, width = acts_hbm.shape
    image_rows = blocks.shape[1] // images
    hidden = w_in.shape[1]
    low_len = low.shape[1]
    groups = hidden // low_len
    row_shards = 4
    row = lax.axis_index("rows")
    col = lax.axis_index("cols")
    me_all = col * row_shards + row

    twin = row + 1 - 2 * lax.rem(row, 2)
    far = lax.rem(row + 2, row_shards)
    layer = {"cols": col + 1 - 2 * lax.rem(col, 2)}
    row_peers = [{"rows": lax.rem(row + ahead, row_shards)} for ahead in range(1, row_shards)]
    col_peers = [{"cols": lax.rem(col + ahead, col_shards)} for ahead in range(1, col_shards)]

    barrier = pltpu.get_barrier_semaphore()
    for peer in row_peers + col_peers:
        pl.semaphore_signal(barrier, inc=1, device_id=peer, device_id_type=MESH)

    raw_loads = [
        pltpu.make_async_copy(acts_hbm, raw.at[0], load_sems.at[3]),
        pltpu.make_async_copy(grads_hbm, raw.at[1], load_sems.at[4]),
    ]
    loads = [
        pltpu.make_async_copy(bits_hbm.at[pl.ds(0, bits.shape[0])], bits, load_sems.at[0]),
        pltpu.make_async_copy(w_in_hbm, w_in, load_sems.at[1]),
        pltpu.make_async_copy(w_out_hbm, w_out, load_sems.at[2]),
    ]
    for load in raw_loads + loads[1:] + loads[:1]:
        load.start()
    for load in raw_loads:
        load.wait()

    own_cols = pl.ds(pl.multiple_of(row * width, LANES), width)
    gap = jnp.zeros((image_rows - tokens, width), jnp.bfloat16)
    for image in range(images):
        for kind in range(2):
            blocks[kind, image * image_rows : (image + 1) * image_rows, own_cols] = (
                jnp.concatenate([raw[kind, image], gap], axis=0)
            )
    pl.semaphore_wait(barrier, len(row_peers) + len(col_peers))

    tiles = image_rows // 16
    count = far_sems.shape[1]
    per_image = count // images
    edges = [
        image * image_rows + 16 * (tiles * part // per_image)
        for image in range(images)
        for part in range(per_image)
    ] + [images * image_rows]

    def place(kind, owner, part):
        rows = pl.ds(0, images * image_rows)
        if part is not None:
            rows = pl.ds(edges[part], edges[part + 1] - edges[part])
        return blocks.at[kind, rows, pl.ds(pl.multiple_of(owner * width, LANES), width)]

    def send(ref, sems, at, partner):
        return pltpu.make_async_remote_copy(
            src_ref=ref,
            dst_ref=ref,
            send_sem=sems.at[0, at],
            recv_sem=sems.at[1, at],
            device_id=partner,
            device_id_type=MESH,
        )

    mine = lax.rem(col, 2)
    to_far = [send(place(mine, row, part), far_sems, part, {"rows": far}) for part in range(count)]
    to_twin = [send(place(kind, row, None), twin_sems, kind, {"rows": twin}) for kind in range(2)]
    to_layer = [send(place(mine, far, part), layer_sems, part, layer) for part in range(count)]
    pass_far = [
        send(place(mine, far, part), pass_far_sems, part, {"rows": twin}) for part in range(count)
    ]
    pass_layer = [
        send(place(1 - mine, far, part), pass_layer_sems, part, {"rows": twin})
        for part in range(count)
    ]
    for copy in to_far + to_twin:
        copy.start()

    def relay_far(part):
        to_far[part].wait_recv()
        to_layer[part].start()
        pass_far[part].start()

    def relay_layer(part):
        to_layer[part].wait_recv()
        pass_layer[part].start()

    lane = lax.broadcasted_iota(jnp.int32, (LANES, LANES), 1)

    def make_signs(at, _):
        column = jnp.broadcast_to(picks_ref[pl.ds(at, 1), :], (LANES, LANES)).T
        inside = jnp.bitwise_and(column, local_len - 1)
        upper = jnp.right_shift(inside, low_len.bit_length() - 1)
        lower = jnp.bitwise_and(inside, low_len - 1)
        rows = pl.ds(pl.multiple_of(at * LANES, LANES), LANES)
        for group in range(groups):
            for tile in range(width // LANES):
                spot = groups * (lane + tile * LANES) + group
                start = group * width + tile * LANES
                high[rows, start : start + LANES] = signs_of(upper, spot).astype(jnp.bfloat16)
        for tile in range(low_len // LANES):
            low[rows, tile * LANES : (tile + 1) * LANES] = signs_of(
                lower, lane + tile * LANES
            ).astype(jnp.bfloat16)
        return 0

    def signs(part):
        every = picks_ref.shape[0]
        lax.fori_loop(every * part // 8, every * (part + 1) // 8, make_signs, 0)

    pair = 2 * width

    every_row = slice(0, images * image_rows)

    def products(rows, half, group):
        cols = slice(group * low_len, (group + 1) * low_len)
        part = pl.ds(pl.multiple_of(half * pair, LANES), pair)
        pre = jnp.dot(blocks[0, rows, part], w_in[part, cols], preferred_element_type=jnp.float32)
        back = lax.dot_general(
            blocks[1, rows, part],
            w_out[cols, part],
            (((1,), (1,)), ((), ())),
            preferred_element_type=jnp.float32,
        )
        return pre, back

    here = row // 2

    def own_products(group):
        cols = slice(group * low_len, (group + 1) * low_len)
        pre, back = products(every_row, here, group)
        pre_sum[:, cols] = pre + bias_ref[:, cols].astype(jnp.float32)
        back_sum[:, cols] = back

    def image_signed(image):
        rows = slice(image * image_rows, (image + 1) * image_rows)
        for group in range(groups):
            cols = slice(group * low_len, (group + 1) * low_len)
            pre, back = products(rows, 1 - here, group)
            pre = pre + pre_sum[rows, cols]
            back = back + back_sum[rows, cols]
            pre_grad = (back * gelu_slope(pre)).astype(jnp.bfloat16)
            grad = lax.dot_general(
                blocks[0, rows, own_cols],
                pre_grad,
                (((0,), (0,)), ((), ())),
                preferred_element_type=jnp.float32,
            )
            for tile in range(low_len // LANES):
                first = group * (low_len // LANES) + tile
                flips = bits[pl.ds(first, width, stride=hidden // LANES), :]
                piece = grad[:, tile * LANES : (tile + 1) * LANES]
                signed[
                    image,
                    group * width : (group + 1) * width,
                    tile * LANES : (tile + 1) * LANES,
                ] = (piece * (1 - 2 * flips).astype(jnp.float32)).astype(jnp.bfloat16)

    scale = 1.0 / math.sqrt(local_len * col_shards * row_shards)
    step = 512
    halves = 2
    unit_rows = picks_ref.shape[0] // halves

    def select(image, half):
        def one(at, _):
            rows = pl.ds(pl.multiple_of(at * step, step), step)
            weight = low[rows, :].astype(jnp.float32)
            found = jnp.dot(high[rows, :], signed[image], preferred_element_type=jnp.float32)
            total = jnp.zeros((step, LANES), jnp.float32)
            for tile in range(low_len // LANES):
                cols = slice(tile * LANES, (tile + 1) * LANES)
                total = total + found[:, cols] * weight[:, cols]
            for part in range(step // LANES):
                block = total[part * LANES : (part + 1) * LANES].T
                mixed[image, pl.ds(at * (step // LANES) + part, 1), :] = jnp.sum(
                    block, axis=0, keepdims=True
                )
            return 0

        steps = unit_rows * LANES // step
        lax.fori_loop(half * steps, (half + 1) * steps, one, 0)
        rows = slice(half * unit_rows, (half + 1) * unit_rows)
        owner = jnp.right_shift(picks_ref[rows, :], local_len.bit_length() - 1)
        facing = signs_of(owner, jnp.broadcast_to(me_all, owner.shape)) * scale
        return mixed[image, rows, :] * facing

    def exchange(slots, sems, unit, me, peers):
        return [
            pltpu.make_async_remote_copy(
                src_ref=slots.at[unit, me],
                dst_ref=slots.at[unit, me],
                send_sem=sems.at[0, unit, at],
                recv_sem=sems.at[1, unit, at],
                device_id=peer,
                device_id_type=MESH,
            )
            for at, peer in enumerate(peers)
        ]

    def landed(slots, unit):
        total = slots[unit, 0]
        for at in range(1, slots.shape[1]):
            total = total + slots[unit, at]
        return total

    units = images * halves
    by_row = [exchange(row_slots, row_sems, unit, row, row_peers) for unit in range(units)]
    by_col = [exchange(col_slots, col_sems, unit, col, col_peers) for unit in range(units)]

    def sum_rows(unit, value):
        row_slots[unit, row] = value
        for copy in by_row[unit]:
            copy.start()

    def sum_cols(unit):
        for copy in by_row[unit]:
            copy.wait_recv()
        col_slots[unit, col] = landed(row_slots, unit)
        for copy in by_col[unit]:
            copy.start()

    def finish(unit):
        for copy in by_col[unit]:
            copy.wait_recv()
        image, half = divmod(unit, halves)
        out_ref[image, half * unit_rows : (half + 1) * unit_rows, :] = landed(col_slots, unit)

    signs(0)
    signs(1)
    signs(2)
    relay_far(0)
    signs(3)
    relay_far(1)
    signs(4)
    for load in loads[1:]:
        load.wait()
    for copy in to_twin:
        copy.wait_recv()
    own_products(0)
    relay_far(2)
    relay_layer(0)
    signs(5)
    signs(6)
    relay_layer(1)
    relay_far(3)
    own_products(1)
    relay_layer(2)
    own_products(2)
    relay_far(4)
    signs(7)
    loads[0].wait()
    for copy in pass_far[:per_image] + pass_layer[:per_image]:
        copy.wait_recv()
    relay_layer(3)
    image_signed(0)
    relay_far(5)
    relay_layer(4)
    value = select(0, 0)
    relay_layer(5)
    sum_rows(0, value)
    value = select(0, 1)
    sum_cols(0)
    sum_rows(1, value)
    for copy in pass_far[per_image:] + pass_layer[per_image:]:
        copy.wait_recv()
    image_signed(1)
    finish(0)
    sum_cols(1)
    value = select(1, 0)
    finish(1)
    sum_rows(2, value)
    value = select(1, 1)
    sum_rows(3, value)
    sum_cols(2)
    sum_cols(3)
    finish(2)
    finish(3)
    for copy in to_far + to_twin + to_layer + pass_far + pass_layer:
        copy.wait_send()
    for unit in range(units):
        for copy in by_row[unit] + by_col[unit]:
            copy.wait_send()


def body(acts, out_grad, w_in, bias_in, w_out, sign_bits, picks):
    images, tokens, width = acts.shape
    hidden = w_in.shape[1]
    low_len = low_part(hidden)
    row_shards = lax.axis_size("rows")
    col_shards = lax.axis_size("cols")
    fits = low_len % LANES == 0 and width % LANES == 0 and picks.shape[0] % (16 * LANES) == 0
    if not fits or row_shards != 4 or col_shards % 2 or images != 2 or hidden != 3 * low_len:
        return plain_body(acts, out_grad, w_in, bias_in, w_out, sign_bits, picks)
    local_len = sign_bits.shape[0]
    padded = -(-tokens // 16) * 16
    groups = hidden // low_len
    count = picks.shape[0]
    parts = 6
    halves = 2
    units = images * halves
    slot = (count // LANES // halves, LANES)
    sketch_shape = (images, count // LANES, LANES)
    vmem = pl.BlockSpec(memory_space=pltpu.VMEM)
    anywhere = pl.BlockSpec(memory_space=pl.ANY)
    sketch = pl.pallas_call(
        functools.partial(kernel, local_len, col_shards),
        out_shape=jax.ShapeDtypeStruct(sketch_shape, jnp.float32),
        in_specs=[anywhere, anywhere, anywhere, vmem, anywhere, anywhere, vmem],
        out_specs=vmem,
        scratch_shapes=[
            pltpu.VMEM((2,) + acts.shape, jnp.bfloat16),
            pltpu.VMEM((2, images * padded, row_shards * width), jnp.bfloat16),
            pltpu.VMEM(w_in.shape, jnp.bfloat16),
            pltpu.VMEM(w_out.shape, jnp.bfloat16),
            pltpu.VMEM((width * hidden // LANES, LANES), jnp.int32),
            pltpu.VMEM((count, groups * width), jnp.bfloat16),
            pltpu.VMEM((count, low_len), jnp.bfloat16),
            pltpu.VMEM((images, groups * width, low_len), jnp.bfloat16),
            pltpu.VMEM((images * padded, hidden), jnp.float32),
            pltpu.VMEM((images * padded, hidden), jnp.float32),
            pltpu.VMEM(sketch_shape, jnp.float32),
            pltpu.VMEM((units, row_shards) + slot, jnp.float32),
            pltpu.VMEM((units, col_shards) + slot, jnp.float32),
            pltpu.SemaphoreType.DMA((5,)),
            pltpu.SemaphoreType.DMA((2, 2)),
            pltpu.SemaphoreType.DMA((2, parts)),
            pltpu.SemaphoreType.DMA((2, parts)),
            pltpu.SemaphoreType.DMA((2, parts)),
            pltpu.SemaphoreType.DMA((2, parts)),
            pltpu.SemaphoreType.DMA((2, units, row_shards - 1)),
            pltpu.SemaphoreType.DMA((2, units, col_shards - 1)),
        ],
        compiler_params=pltpu.CompilerParams(
            vmem_limit_bytes=56 * 2**20, collective_id=0, has_side_effects=True
        ),
    )(
        acts,
        out_grad,
        w_in,
        bias_in.reshape(1, hidden),
        w_out,
        sign_bits.reshape(local_len // LANES, LANES),
        picks.reshape(count // LANES, LANES),
    )
    return sketch.reshape(images, count)


def solution(mesh):
    return jax.shard_map(
        body,
        mesh=mesh,
        in_specs=(
            P("groups", None, "rows"),
            P("groups", None, "rows"),
            P(None, "cols"),
            P("cols"),
            P("cols", None),
            P(("cols", "rows")),
            P(),
        ),
        out_specs=P("groups", None),
        check_vma=False,
    )
```

time: 58.5 us -> 55.3 us (0.945)
  Pallas kernels: 52 us -> 48.7 us
    pallas_call x1, Pallas kernels: 52 us -> 48.7 us  [body(): pl.pallas_call(functools.partial(kernel, local_len, col_shards), out_shap...]
where the time goes in v2:
time: 55.3 us; the launch traced here: 54.9 us
  Pallas kernels  48.7 us (88%)
  local copies, waits for them, and re-layouts  6.26 us (11%)
    pallas_call x1, Pallas kernels, body(): pl.pallas_call(functools.partial(kernel, local_len, col_shards), out_shap...  48.7 us
    unnamed x3, local copies, waits for them, and re-layouts  4.97 us
    reshape x1, local copies, waits for them, and re-layouts, body(): bias_in.reshape(1, hidden)  1.28 us

profile of v2, /device:TPU:0, one launch (start us, length us, event | category | flops | bytes accessed | tf_op | source)
XLA Modules:
  0.0 54.9 jit_solution(18023840804994449604)
XLA Ops:
  0.0 1.3 %reshape.12.bias_ref = bf16[1,1536]{1,0:T(2,128)(2,1)} reshape(bf16[1536]{0:T(1024)(128)(2,1)} %param.10) | data formatting | bytes 6144 | tf_op jit(solution)/shard_map/reshape | solution.py:435
  1.3 1.8 %copy.8.acts_hbm = bf16[2,257,384]{2,1,0:T(8,128)(2,1)} copy(bf16[2,257,384]{2,0,1:T(2,128)(2,1)} %param.7) | data formatting | bytes 789504 | tf_op args[0]
  3.1 1.8 %copy.9.grads_hbm = bf16[2,257,384]{2,1,0:T(8,128)(2,1)} copy(bf16[2,257,384]{2,0,1:T(2,128)(2,1)} %param.8) | data formatting | bytes 789504 | tf_op args[1]
  4.9 48.7 %shard_map.73 = f32[2,32,128]{2,1,0:T(8,128)} custom-call(bf16[2,257,384]{2,1,0:T(8,128)(2,1)} %copy.8.acts_hbm, bf16[2,257,384]{2,1,0:T(8,128)(2,1)} %copy.9.grads_hbm, bf16[1536,1536]{1,0:T(8,128)(2,1)} %w_in_hbm.1, bf16[1,1536]{1,0:T(2,128)(2,1)} %reshape.12.bias_ref, bf16[1536,1536]{1,0:T(8,128)(2,1)} %w_out_hbm.1, s32[8192,128]{1,0:T(8,128)} %bitcast.6, ...), custom_call_target="tpu_custom_call" | custom-call | tf_op jit(solution)/shard_map/pallas_call | solution.py:400
  53.5 1.4 %copy.12 = f32[1,2,32,128]{3,1,2,0:T(2,128)} copy(f32[1,2,32,128]{3,2,1,0:T(8,128)} %bitcast.7) | data formatting | bytes 65536

commit v3 on v2

--- a/solution.py
+++ b/solution.py
@@ -89,7 +89,7 @@
     row_sems,
     col_sems,
 ):
-    images, tokens, width = acts_hbm.shape
+    tokens, images, width = acts_hbm.shape
     image_rows = blocks.shape[1] // images
     hidden = w_in.shape[1]
     low_len = low.shape[1]
@@ -128,7 +128,7 @@
     for image in range(images):
         for kind in range(2):
             blocks[kind, image * image_rows : (image + 1) * image_rows, own_cols] = (
-                jnp.concatenate([raw[kind, image], gap], axis=0)
+                jnp.concatenate([raw[kind, :, image, :], gap], axis=0)
             )
     pl.semaphore_wait(barrier, len(row_peers) + len(col_peers))
 
@@ -224,7 +224,12 @@
     def own_products(group):
         cols = slice(group * low_len, (group + 1) * low_len)
         pre, back = products(every_row, here, group)
-        pre_sum[:, cols] = pre + bias_ref[:, cols].astype(jnp.float32)
+        offsets = bias_ref[...].astype(jnp.float32)
+        for tile in range(low_len // LANES):
+            at = group * (low_len // LANES) + tile
+            pre_sum[:, at * LANES : (at + 1) * LANES] = (
+                pre[:, tile * LANES : (tile + 1) * LANES] + offsets[at : at + 1, :]
+            )
         back_sum[:, cols] = back
 
     def image_signed(image):
@@ -252,7 +257,7 @@
                 ] = (piece * (1 - 2 * flips).astype(jnp.float32)).astype(jnp.bfloat16)
 
     scale = 1.0 / math.sqrt(local_len * col_shards * row_shards)
-    step = 512
+    step = 8 * LANES
     halves = 2
     unit_rows = picks_ref.shape[0] // halves
 
@@ -403,7 +408,7 @@
         in_specs=[anywhere, anywhere, anywhere, vmem, anywhere, anywhere, vmem],
         out_specs=vmem,
         scratch_shapes=[
-            pltpu.VMEM((2,) + acts.shape, jnp.bfloat16),
+            pltpu.VMEM((2, tokens, images, width), jnp.bfloat16),
             pltpu.VMEM((2, images * padded, row_shards * width), jnp.bfloat16),
             pltpu.VMEM(w_in.shape, jnp.bfloat16),
             pltpu.VMEM(w_out.shape, jnp.bfloat16),
@@ -429,10 +434,10 @@
             vmem_limit_bytes=56 * 2**20, collective_id=0, has_side_effects=True
         ),
     )(
-        acts,
-        out_grad,
+        acts.transpose(1, 0, 2),
+        out_grad.transpose(1, 0, 2),
         w_in,
-        bias_in.reshape(1, hidden),
+        bias_in.reshape(hidden // LANES, LANES),
         w_out,
         sign_bits.reshape(local_len // LANES, LANES),
         picks.reshape(count // LANES, LANES),

time: 55.3 us -> 49.6 us (0.90)
  local copies, waits for them, and re-layouts: 6.26 us -> 1.4 us
  Pallas kernels: 48.7 us -> 47.9 us
    unnamed x3 -> x1, local copies, waits for them, and re-layouts: 4.97 us -> 1.4 us
    reshape x1 -> x0, local copies, waits for them, and re-layouts: 1.28 us -> none  [body(): bias_in.reshape(1, hidden)]
    pallas_call x1, Pallas kernels: 48.7 us -> 47.9 us  [body(): pl.pallas_call(functools.partial(kernel, local_len, col_shards), out_shap...]
where the time goes in v3:
time: 49.6 us; the launch traced here: 49.4 us
  Pallas kernels  47.9 us (97%)
  local copies, waits for them, and re-layouts  1.4 us (3%)
    pallas_call x1, Pallas kernels, body(): pl.pallas_call(functools.partial(kernel, local_len, col_shards), out_shap...  47.9 us
    unnamed x1, local copies, waits for them, and re-layouts  1.4 us

profile of v3, /device:TPU:0, one launch (start us, length us, event | category | flops | bytes accessed | tf_op | source)
XLA Modules:
  0.0 49.4 jit_solution(8825916295141171941)
XLA Ops:
  0.0 47.9 %shard_map.73 = f32[2,32,128]{2,1,0:T(8,128)} custom-call(bf16[257,2,384]{2,1,0:T(2,128)(2,1)} %bitcast.10, bf16[257,2,384]{2,1,0:T(2,128)(2,1)} %bitcast.11, bf16[1536,1536]{1,0:T(8,128)(2,1)} %w_in_hbm.1, bf16[12,128]{1,0:T(8,128)(2,1)} %bitcast.14, bf16[1536,1536]{1,0:T(8,128)(2,1)} %w_out_hbm.1, s32[8192,128]{1,0:T(8,128)} %bitcast.9, s32[32,128]{1,0:T(8,128)} %bitcast.13), custom_call_target="tpu_custom_call" | custom-call | tf_op jit(solution)/shard_map/pallas_call | solution.py:405
  48.0 1.4 %copy.10 = f32[1,2,32,128]{3,1,2,0:T(2,128)} copy(f32[1,2,32,128]{3,2,1,0:T(8,128)} %bitcast.12) | data formatting | bytes 65536

commit v4 on v3

--- a/solution.py
+++ b/solution.py
@@ -232,9 +232,9 @@
             )
         back_sum[:, cols] = back
 
-    def image_signed(image):
+    def image_signed(image, wanted):
         rows = slice(image * image_rows, (image + 1) * image_rows)
-        for group in range(groups):
+        for group in wanted:
             cols = slice(group * low_len, (group + 1) * low_len)
             pre, back = products(rows, 1 - here, group)
             pre = pre + pre_sum[rows, cols]
@@ -344,15 +344,17 @@
     relay_layer(1)
     relay_far(3)
     own_products(1)
+    own_products(2)
+    signs(7)
     relay_layer(2)
-    own_products(2)
-    relay_far(4)
-    signs(7)
     loads[0].wait()
     for copy in pass_far[:per_image] + pass_layer[:per_image]:
         copy.wait_recv()
+    image_signed(0, [0])
+    relay_far(4)
+    image_signed(0, [1])
     relay_layer(3)
-    image_signed(0)
+    image_signed(0, [2])
     relay_far(5)
     relay_layer(4)
     value = select(0, 0)
@@ -363,7 +365,7 @@
     sum_rows(1, value)
     for copy in pass_far[per_image:] + pass_layer[per_image:]:
         copy.wait_recv()
-    image_signed(1)
+    image_signed(1, range(groups))
     finish(0)
     sum_cols(1)
     value = select(1, 0)

time: 49.6 us -> 50.7 us (1.022)
  Pallas kernels: 47.9 us -> 49 us
    pallas_call x1, Pallas kernels: 47.9 us -> 49 us  [body(): pl.pallas_call(functools.partial(kernel, local_len, col_shards), out_shap...]
where the time goes in v4:
time: 50.7 us; the launch traced here: 50.4 us
  Pallas kernels  49 us (97%)
  local copies, waits for them, and re-layouts  1.4 us (3%)
    pallas_call x1, Pallas kernels, body(): pl.pallas_call(functools.partial(kernel, local_len, col_shards), out_shap...  49 us
    unnamed x1, local copies, waits for them, and re-layouts  1.4 us

profile of v4, /device:TPU:0, one launch (start us, length us, event | category | flops | bytes accessed | tf_op | source)
XLA Modules:
  0.0 50.4 jit_solution(10723113446677601810)
XLA Ops:
  0.0 49.0 %shard_map.73 = f32[2,32,128]{2,1,0:T(8,128)} custom-call(bf16[257,2,384]{2,1,0:T(2,128)(2,1)} %bitcast.10, bf16[257,2,384]{2,1,0:T(2,128)(2,1)} %bitcast.11, bf16[1536,1536]{1,0:T(8,128)(2,1)} %w_in_hbm.1, bf16[12,128]{1,0:T(8,128)(2,1)} %bitcast.14, bf16[1536,1536]{1,0:T(8,128)(2,1)} %w_out_hbm.1, s32[8192,128]{1,0:T(8,128)} %bitcast.9, s32[32,128]{1,0:T(8,128)} %bitcast.13), custom_call_target="tpu_custom_call" | custom-call | tf_op jit(solution)/shard_map/pallas_call | solution.py:407
  49.0 1.4 %copy.10 = f32[1,2,32,128]{3,1,2,0:T(2,128)} copy(f32[1,2,32,128]{3,2,1,0:T(8,128)} %bitcast.12) | data formatting | bytes 65536
